TPU v7x, 512 devices: a whole 4x4x16 slice. The times are simulated.
512 devices in a mesh: pm: 2 (over y_lo), ka: 128 (over x, z, core), isdf: 2 (over y_hi).
Axes of the slice: x: 4, y: 4 (y_hi: 2, y_lo: 2; y = y_hi * 2 + y_lo), z: 16, core: 2. Of those that a mesh axis runs over, the one named last changes fastest.
Arguments:
- amplitudes: bfloat16 [2, 2, 2, 256, 64, 256], P('pm', None, None, 'ka'), may hold values from -6 to 6
- conduction: bfloat16 [2, 256, 256, 512], P(None, 'ka', None, 'isdf'), may hold values from -0.375 to 0.375
- valence: bfloat16 [2, 256, 64, 512], P(None, 'ka'), may hold values from -0.75 to 0.75
- energy: float32 [256, 64, 256], P('ka', None, 'isdf'), may hold values from 0.5 to 2.5
- screened: bfloat16 [4, 2, 512, 512], P(None, None, 'isdf'), may hold values from -0.59765625 to 0.59765625
- coulomb: float32 [512, 512], P(None, 'isdf'), may hold values from -0.03125 to 0.03125
- mirror: int32 [256], P('ka'), may hold values from 0 to 255, as said below
- transfer_class: int32 [256, 256], P('ka'), may hold values from 0 to 3, as said below
Outputs:
- response: bfloat16 [2, 2, 2, 256, 64, 256], P('pm', None, None, 'ka', None, 'isdf')
Inputs may be any that keep to these rules, and one draw needn't show every extreme that they name: mirror[mirror[k]] = k; a k-point of block j (the aligned block of 2 k-points that holds it) has its mirror in block 127 - j. transfer_class[k, k2] depends only on (k - k2) mod 256.
All inputs are finite; a program needn't handle non-finite values.
Results may differ from a plain program's by a relative error of at most 0.015.
Values may be sent and summed in bfloat16 or wider, within the bound.
A program may use at most 128 MiB of HBM per device.

v0:
```python
import jax
import jax.numpy as jnp
from jax import lax
from jax.sharding import PartitionSpec as P

REACH = 2
HIGHEST = lax.Precision.HIGHEST


def swapped(block, axis, apart):
    count = lax.axis_size(axis)
    route = []
    for low in range(count):
        high = low | 1 << apart
        if high != low and high < count:
            route += [(low, high), (high, low)]
    return lax.ppermute(block, axis, route)


def shifted(value, axis, by):
    size = lax.axis_size(axis)
    return lax.ppermute(value, axis, [(i, (i + by) % size) for i in range(size)])


def pair_einsum(pattern, left, right, conjugate):

    def single(first, second):
        return jnp.einsum(pattern, first, second, preferred_element_type=jnp.float32)

    if conjugate:
        real_part = single(left[0], right[0]) + single(left[1], right[1])
        imag_part = single(left[1], right[0]) - single(left[0], right[1])
    else:
        real_part = single(left[0], right[0]) - single(left[1], right[1])
        imag_part = single(left[0], right[1]) + single(left[1], right[0])
    return (real_part, imag_part)


def conjugated(field):
    return jnp.stack([field[:, 0], -field[:, 1]], axis=1)


def coefficients(vector, conduction):
    real_part, imag_part = pair_einsum(
        "bkvc,kcm->bkvm", (vector[:, 0], vector[:, 1]), (conduction[0], conduction[1]), False
    )
    return jnp.stack([real_part, imag_part], axis=1).astype(jnp.bfloat16)


def amp_bits(field):
    for bit_number in range(lax.axis_size("ka").bit_length() - 1):
        field = swapped(field, "ka", bit_number)
    return field


def result_bits(field):
    for bit_number in range(lax.axis_size("ka").bit_length() - 1):
        field = swapped(field, "ka", bit_number)
    return field


def per_device(amplitudes, conduction, valence, energy, screened, coulomb, mirror, transfer_class):
    pm_index = lax.axis_index("pm")
    ka_index = lax.axis_index("ka")
    isdf_index = lax.axis_index("isdf")
    ka_count = lax.axis_size("ka")
    kpoint_count = conduction.shape[1]
    mu_count = conduction.shape[3]
    point_count = valence.shape[3]
    cond_share = energy.shape[2]
    vector_count = amplitudes.shape[1]
    is_plus = pm_index == 0
    parity = jnp.where(is_plus, 1.0, -1.0).astype(jnp.float32)
    exchange_weight = jnp.where(is_plus, 4.0, 0.0).astype(jnp.float32)
    local_amps = amplitudes[0]
    partner_amps = swapped(local_amps, "pm", 0)
    partner_side = jnp.where(is_plus, partner_amps, local_amps)
    distant_side = amp_bits(partner_side)
    direct = jnp.where(is_plus, local_amps, partner_amps).astype(jnp.float32)
    local_mirror = mirror - (ka_count - 1 - ka_index) * kpoint_count
    flipped = conjugated(jnp.take(distant_side, local_mirror, axis=2).astype(jnp.float32))
    vector = (direct + parity * flipped).astype(jnp.bfloat16)
    own_coef = coefficients(vector, conduction)
    valence_part = lax.dynamic_slice_in_dim(valence, isdf_index * mu_count, mu_count, 3)
    rho_real = jnp.einsum(
        "kvm,bkvm->bm", valence_part[0], own_coef[:, 0], preferred_element_type=jnp.float32
    )
    rho_real = rho_real + jnp.einsum(
        "kvm,bkvm->bm", valence_part[1], own_coef[:, 1], preferred_element_type=jnp.float32
    )
    rho_imag = jnp.einsum(
        "kvm,bkvm->bm", valence_part[0], own_coef[:, 1], preferred_element_type=jnp.float32
    )
    rho_imag = rho_imag - jnp.einsum(
        "kvm,bkvm->bm", valence_part[1], own_coef[:, 0], preferred_element_type=jnp.float32
    )
    density = jnp.stack([rho_real, rho_imag], axis=1)
    spread = jnp.einsum("nm,brm->brn", coulomb, density, precision=HIGHEST)
    spread = lax.psum(spread, ("ka", "isdf"))
    potential = lax.dynamic_slice_in_dim(spread, isdf_index * mu_count, mu_count, 2)
    class_ids = jnp.arange(screened.shape[0], dtype=jnp.int32)

    def accumulate(totals, coef_block, valence_block, source):
        pair_real, pair_imag = pair_einsum(
            "bqvm,qvn->bqmn",
            (coef_block[:, 0], coef_block[:, 1]),
            (valence_block[0], valence_block[1]),
            True,
        )
        pair_real = pair_real.astype(jnp.bfloat16)
        pair_imag = pair_imag.astype(jnp.bfloat16)
        classes = lax.dynamic_slice_in_dim(transfer_class, source * kpoint_count, kpoint_count, 1)
        selector = (classes[:, :, None] == class_ids).astype(jnp.bfloat16)
        total_real, total_imag = totals
        for visitor in range(kpoint_count):
            chosen = jnp.einsum(
                "kw,wrmn->rkmn", selector[:, visitor], screened, preferred_element_type=jnp.float32
            ).astype(jnp.bfloat16)
            screen_real = chosen[0][None].astype(jnp.float32)
            screen_imag = chosen[1][None].astype(jnp.float32)
            visit_real = pair_real[:, visitor][:, None].astype(jnp.float32)
            visit_imag = pair_imag[:, visitor][:, None].astype(jnp.float32)
            total_real = total_real + (screen_real * visit_real - screen_imag * visit_imag)
            total_imag = total_imag + (screen_real * visit_imag + screen_imag * visit_real)
        return (total_real, total_imag)

    payload = (vector, conduction, valence)

    def advance(moving, offset):
        return shifted((moving[0], moving[1], moving[2]), "ka", offset)

    def unpack(moving):
        return (coefficients(moving[0], moving[1]), moving[2])

    def visit(totals, moving, distance):
        coef_block, valence_block = unpack(moving)
        source = jnp.mod(ka_index + distance, ka_count)
        return accumulate(totals, coef_block, valence_block, source)

    zero_field = jnp.zeros((vector_count, kpoint_count, mu_count, point_count), jnp.float32)
    totals = accumulate((zero_field, zero_field), own_coef, valence, ka_index)
    below_item = payload
    for count_done in range(REACH):
        below_item = advance(below_item, 1)
        totals = visit(totals, below_item, -(count_done + 1))
    above_item = payload
    for count_done in range(REACH):
        above_item = advance(above_item, -1)
        totals = visit(totals, above_item, count_done + 1)
    sum_real = totals[0].astype(jnp.bfloat16)
    sum_imag = totals[1].astype(jnp.bfloat16)
    back_real, back_imag = pair_einsum(
        "bkmn,kvn->bkvm", (sum_real, sum_imag), (valence[0], valence[1]), False
    )
    potential_real = potential[:, 0][:, None, None, :]
    potential_imag = potential[:, 1][:, None, None, :]
    exchange_real = potential_real * valence_part[0] - potential_imag * valence_part[1]
    exchange_imag = potential_real * valence_part[1] + potential_imag * valence_part[0]
    field_real = (exchange_weight * exchange_real - back_real).astype(jnp.bfloat16)
    field_imag = (exchange_weight * exchange_imag - back_imag).astype(jnp.bfloat16)
    out_real, out_imag = pair_einsum(
        "bkvm,kcm->bkvc", (field_real, field_imag), (conduction[0], conduction[1]), True
    )
    partial_out = jnp.stack([out_real, out_imag], axis=1)
    summed = lax.psum_scatter(
        partial_out.astype(jnp.bfloat16), "isdf", scatter_dimension=4, tiled=True
    ).astype(jnp.float32)
    vector_part = lax.dynamic_slice_in_dim(vector, isdf_index * cond_share, cond_share, 4).astype(
        jnp.float32
    )
    channel_out = (energy[None, None] * vector_part + summed).astype(jnp.bfloat16)
    partner_out = swapped(channel_out, "pm", 0)
    blended = (
        0.5 * (partner_out.astype(jnp.float32) + parity * channel_out.astype(jnp.float32))
    ).astype(jnp.bfloat16)
    distant_out = result_bits(blended)
    reflected = conjugated(jnp.take(distant_out, local_mirror, axis=2))
    result = jnp.where(is_plus, blended, reflected)
    return result[None]


def solution(mesh):
    return jax.shard_map(
        per_device,
        mesh=mesh,
        in_specs=(
            P("pm", None, None, "ka", None, None),
            P(None, "ka", None, "isdf"),
            P(None, "ka", None, None),
            P("ka", None, "isdf"),
            P(None, None, "isdf", None),
            P(None, "isdf"),
            P("ka"),
            P("ka", None),
        ),
        out_specs=P("pm", None, None, "ka", None, "isdf"),
        check_vma=False,
    )
```

profile of v0, /device:TPU:2, one launch (start us, length us, event | category | flops | bytes accessed | tf_op | source)
XLA Modules:
  0.0 1090.2 jit_solution(7875653439164302398)
XLA Ops:
  8.6 10.8 collective-permute-start.15
  21.3 5.8 collective-permute-start.16
  76.7 6.6 collective-permute-done.2
  87.2 12.3 %collective-permute-done.3 = bf16[2,2,2,64,256]{4,3,0,2,1:T(8,128)(2,1)S(1)} collective-permute-done((bf16[2,2,2,64,256]{4,3,0,2,1:T(8,128)(2,1)S(1)}, bf16[2,2,2,64,256]{4,3,0,2,1:T(8,128)(2,1)S(1)}, u32[]{:S(2)}, u32[]{:S(2)}) %collective-permute-start.3) | collective-permute-done | bytes 262176 | tf_op jit(solution)/shard_map/ppermute | solution.py:17
  104.0 22.7 %collective-permute-done.4 = bf16[2,2,2,64,256]{4,3,0,2,1:T(8,128)(2,1)S(1)} collective-permute-done((bf16[2,2,2,64,256]{4,3,0,2,1:T(8,128)(2,1)S(1)}, bf16[2,2,2,64,256]{4,3,0,2,1:T(8,128)(2,1)S(1)}, u32[]{:S(2)}, u32[]{:S(2)}) %collective-permute-start.4) | collective-permute-done | bytes 262176 | tf_op jit(solution)/shard_map/ppermute | solution.py:17
  126.6 14.7 %collective-permute-start.5 = (bf16[2,2,2,64,256]{4,3,0,2,1:T(8,128)(2,1)S(1)}, bf16[2,2,2,64,256]{4,3,0,2,1:T(8,128)(2,1)S(1)}, u32[]{:S(2)}, u32[]{:S(2)}) collective-permute-start(bf16[2,2,2,64,256]{4,3,0,2,1:T(8,128)(2,1)S(1)} %collective-permute-done.4), channel_id=1, source_target_pairs={{0,32},{32,0},{2,34},{34,2},{4,36},{36,4},{6,38},{38,6},{8,40},{40... | collective-permute-start | bytes 786440 | tf_op jit(solution)/shard_map/ppermute | solution.py:17
  143.4 14.8 %collective-permute-done.5 = bf16[2,2,2,64,256]{4,3,0,2,1:T(8,128)(2,1)S(1)} collective-permute-done((bf16[2,2,2,64,256]{4,3,0,2,1:T(8,128)(2,1)S(1)}, bf16[2,2,2,64,256]{4,3,0,2,1:T(8,128)(2,1)S(1)}, u32[]{:S(2)}, u32[]{:S(2)}) %collective-permute-start.5) | collective-permute-done | bytes 262176 | tf_op jit(solution)/shard_map/ppermute | solution.py:17
  163.1 5.4 collective-permute-done.6
  198.8 5.8 collective-permute-start.19
  206.5 5.8 collective-permute-start.18
  228.5 583.0 %psum.7 = f32[2,2,512]{2,1,0:T(2,128)S(1)} all-reduce(f32[2,2,512]{2,1,0:T(2,128)S(1)} %fusion.90), channel_id=1, replica_groups=mesh['pm'=2,'ka'=128,'isdf'=2] {'ka','isdf'}, use_global_device_ids=true, to_apply=%region_0.1 | all-reduce | flops 2048 | bytes 16384 | tf_op jit(solution)/shard_map/psum | solution.py:99
  845.6 5.3 collective-permute-start.17
  878.6 9.2 add_convert_fusion
  887.9 9.5 add_convert_fusion.1
  901.8 92.5 %reduce-scatter.4.cloned.1.call-done = bf16[128,512]{1,0:T(8,128)(2,1)} async-done(((bf16[256,512]{1,0:T(8,128)(2,1)}), bf16[128,512]{1,0:T(8,128)(2,1)}) %reduce-scatter.4.cloned.1.call-update) | async-done | bytes 131088
  999.0 4.7 collective-permute-done.20
  1014.4 4.4 collective-permute-start.23
  1018.9 5.9 collective-permute-done.23
  1024.7 7.6 collective-permute-start.24
  1032.4 9.9 collective-permute-done.24
  1042.2 12.0 %collective-permute-start.25 = (bf16[2,2,2,64,128]{4,3,0,2,1:T(8,128)(2,1)S(1)}, bf16[2,2,2,64,128]{4,3,0,2,1:T(8,128)(2,1)S(1)}, u32[]{:S(2)}, u32[]{:S(2)}) collective-permute-start(bf16[2,2,2,64,128]{4,3,0,2,1:T(8,128)(2,1)S(1)} %collective-permute-done.24), channel_id=1, source_target_pairs={{0,32},{32,0},{2,34},{34,2},{4,36},{36,4},{6,38},{38,6},{8,40},{40... | collective-permute-start | bytes 393224 | tf_op jit(solution)/shard_map/ppermute | solution.py:17
  1054.2 12.1 %collective-permute-done.25 = bf16[2,2,2,64,128]{4,3,0,2,1:T(8,128)(2,1)S(1)} collective-permute-done((bf16[2,2,2,64,128]{4,3,0,2,1:T(8,128)(2,1)S(1)}, bf16[2,2,2,64,128]{4,3,0,2,1:T(8,128)(2,1)S(1)}, u32[]{:S(2)}, u32[]{:S(2)}) %collective-permute-start.25) | collective-permute-done | bytes 131104 | tf_op jit(solution)/shard_map/ppermute | solution.py:17
  1068.8 4.4 collective-permute-done.26
  1077.1 4.4 collective-permute-done.27
  (293 shorter events, 205.7 us)
Async XLA Ops:
  6.5 987.7 %reduce-scatter.4.cloned.1.call-start = ((), (), s32[]{:S(2)}) async-start(), calls=%async_computation.1 | async-start | bytes 393216
  6.5 198.1 %collective-permute-start.9 = (bf16[2,2,256,256]{3,2,1,0:T(8,128)(2,1)}, bf16[2,2,256,256]{3,2,1,0:T(8,128)(2,1)}, u32[]{:S(2)}, u32[]{:S(2)}) collective-permute-start(bf16[2,2,256,256]{3,2,1,0:T(8,128)(2,1)} %param.9), channel_id=1, source_target_pairs={{0,2},{2,4},{4,6},{6,8},{8,10},{10,12},{12,14},{14,16},{16,18},{18... | collective-permute-start | bytes 1572872 | tf_op jit(solution)/shard_map/ppermute | solution.py:22
  8.6 197.9 %collective-permute-start.15 = (bf16[2,2,256,256]{3,2,1,0:T(8,128)(2,1)}, bf16[2,2,256,256]{3,2,1,0:T(8,128)(2,1)}, u32[]{:S(2)}, u32[]{:S(2)}) collective-permute-start(bf16[2,2,256,256]{3,2,1,0:T(8,128)(2,1)} %param.9), channel_id=1, source_target_pairs={{0,254},{2,0},{4,2},{6,4},{8,6},{10,8},{12,10},{14,12},{16,14},{18... | collective-permute-start | bytes 1572872 | tf_op jit(solution)/shard_map/ppermute | solution.py:22
  19.4 177.4 %collective-permute-start.10 = (bf16[2,2,64,512]{3,2,1,0:T(8,128)(2,1)}, bf16[2,2,64,512]{3,2,1,0:T(8,128)(2,1)}, u32[]{:S(2)}, u32[]{:S(2)}) collective-permute-start(bf16[2,2,64,512]{3,2,1,0:T(8,128)(2,1)} %param.10), channel_id=1, source_target_pairs={{0,2},{2,4},{4,6},{6,8},{8,10},{10,12},{12,14},{14,16},{16,18},{18... | collective-permute-start | bytes 786440 | tf_op jit(solution)/shard_map/ppermute | solution.py:22
  21.3 177.5 %collective-permute-start.16 = (bf16[2,2,64,512]{3,2,1,0:T(8,128)(2,1)}, bf16[2,2,64,512]{3,2,1,0:T(8,128)(2,1)}, u32[]{:S(2)}, u32[]{:S(2)}) collective-permute-start(bf16[2,2,64,512]{3,2,1,0:T(8,128)(2,1)} %param.10), channel_id=1, source_target_pairs={{0,254},{2,0},{4,2},{6,4},{8,6},{10,8},{12,10},{14,12},{16,14},{18... | collective-permute-start | bytes 786440 | tf_op jit(solution)/shard_map/ppermute | solution.py:22
  28.1 40.2 %collective-permute-start = (bf16[2,2,2,64,256]{4,3,0,2,1:T(8,128)(2,1)S(1)}, bf16[2,2,2,64,256]{4,3,0,2,1:T(8,128)(2,1)S(1)}, u32[]{:S(2)}, u32[]{:S(2)}) collective-permute-start(bf16[2,2,2,64,256]{4,3,0,2,1:T(8,128)(2,1)S(1)} %bitcast.651), channel_id=1, source_target_pairs={{0,256},{256,0},{1,257},{257,1},{2,258},{258,2},{3,259},{259,3},{4... | collective-permute-start | bytes 786440 | tf_op jit(solution)/shard_map/ppermute | solution.py:17
  72.5 10.7 collective-permute-start.2
  83.2 16.3 %collective-permute-start.3 = (bf16[2,2,2,64,256]{4,3,0,2,1:T(8,128)(2,1)S(1)}, bf16[2,2,2,64,256]{4,3,0,2,1:T(8,128)(2,1)S(1)}, u32[]{:S(2)}, u32[]{:S(2)}) collective-permute-start(bf16[2,2,2,64,256]{4,3,0,2,1:T(8,128)(2,1)S(1)} %collective-permute-done.2), channel_id=1, source_target_pairs={{0,8},{8,0},{2,10},{10,2},{4,12},{12,4},{6,14},{14,6},{16,24},{24,... | collective-permute-start | bytes 786440 | tf_op jit(solution)/shard_map/ppermute | solution.py:17
  99.5 27.1 %collective-permute-start.4 = (bf16[2,2,2,64,256]{4,3,0,2,1:T(8,128)(2,1)S(1)}, bf16[2,2,2,64,256]{4,3,0,2,1:T(8,128)(2,1)S(1)}, u32[]{:S(2)}, u32[]{:S(2)}) collective-permute-start(bf16[2,2,2,64,256]{4,3,0,2,1:T(8,128)(2,1)S(1)} %collective-permute-done.3), channel_id=1, source_target_pairs={{0,16},{16,0},{2,18},{18,2},{4,20},{20,4},{6,22},{22,6},{8,24},{24... | collective-permute-start | bytes 786440 | tf_op jit(solution)/shard_map/ppermute | solution.py:17
  126.6 31.6 %collective-permute-start.5 = (bf16[2,2,2,64,256]{4,3,0,2,1:T(8,128)(2,1)S(1)}, bf16[2,2,2,64,256]{4,3,0,2,1:T(8,128)(2,1)S(1)}, u32[]{:S(2)}, u32[]{:S(2)}) collective-permute-start(bf16[2,2,2,64,256]{4,3,0,2,1:T(8,128)(2,1)S(1)} %collective-permute-done.4), channel_id=1, source_target_pairs={{0,32},{32,0},{2,34},{34,2},{4,36},{36,4},{6,38},{38,6},{8,40},{40... | collective-permute-start | bytes 786440 | tf_op jit(solution)/shard_map/ppermute | solution.py:17
  158.2 10.2 collective-permute-start.6
  168.4 43.9 %collective-permute-start.7 = (bf16[2,2,2,64,256]{4,3,0,2,1:T(8,128)(2,1)}, bf16[2,2,2,64,256]{4,3,0,2,1:T(8,128)(2,1)}, u32[]{:S(2)}, u32[]{:S(2)}) collective-permute-start(bf16[2,2,2,64,256]{4,3,0,2,1:T(8,128)(2,1)} %collective-permute-done.6), channel_id=1, source_target_pairs={{0,128},{128,0},{2,130},{130,2},{4,132},{132,4},{6,134},{134,6},{8... | collective-permute-start | bytes 786440 | tf_op jit(solution)/shard_map/ppermute | solution.py:17
  196.8 658.7 %collective-permute-start.13 = (bf16[2,2,64,512]{3,2,1,0:T(8,128)(2,1)}, bf16[2,2,64,512]{3,2,1,0:T(8,128)(2,1)}, u32[]{:S(2)}, u32[]{:S(2)}) collective-permute-start(bf16[2,2,64,512]{3,2,1,0:T(8,128)(2,1)} %collective-permute-done.10), channel_id=1, source_target_pairs={{0,2},{2,4},{4,6},{6,8},{8,10},{10,12},{12,14},{14,16},{16,18},{18... | collective-permute-start | bytes 786440 | tf_op jit(solution)/shard_map/ppermute | solution.py:22
  198.8 669.1 %collective-permute-start.19 = (bf16[2,2,64,512]{3,2,1,0:T(8,128)(2,1)}, bf16[2,2,64,512]{3,2,1,0:T(8,128)(2,1)}, u32[]{:S(2)}, u32[]{:S(2)}) collective-permute-start(bf16[2,2,64,512]{3,2,1,0:T(8,128)(2,1)} %collective-permute-done.16), channel_id=1, source_target_pairs={{0,254},{2,0},{4,2},{6,4},{8,6},{10,8},{12,10},{14,12},{16,14},{18... | collective-permute-start | bytes 786440 | tf_op jit(solution)/shard_map/ppermute | solution.py:22
  204.6 641.0 %collective-permute-start.12 = (bf16[2,2,256,256]{3,2,1,0:T(8,128)(2,1)}, bf16[2,2,256,256]{3,2,1,0:T(8,128)(2,1)}, u32[]{:S(2)}, u32[]{:S(2)}) collective-permute-start(bf16[2,2,256,256]{3,2,1,0:T(8,128)(2,1)} %collective-permute-done.9), channel_id=1, source_target_pairs={{0,2},{2,4},{4,6},{6,8},{8,10},{10,12},{12,14},{14,16},{16,18},{18... | collective-permute-start | bytes 1572872 | tf_op jit(solution)/shard_map/ppermute | solution.py:22
  206.5 656.7 %collective-permute-start.18 = (bf16[2,2,256,256]{3,2,1,0:T(8,128)(2,1)}, bf16[2,2,256,256]{3,2,1,0:T(8,128)(2,1)}, u32[]{:S(2)}, u32[]{:S(2)}) collective-permute-start(bf16[2,2,256,256]{3,2,1,0:T(8,128)(2,1)} %collective-permute-done.15), channel_id=1, source_target_pairs={{0,254},{2,0},{4,2},{6,4},{8,6},{10,8},{12,10},{14,12},{16,14},{18... | collective-permute-start | bytes 1572872 | tf_op jit(solution)/shard_map/ppermute | solution.py:22
  221.3 594.7 %collective-permute-start.8 = (bf16[2,2,2,64,256]{4,3,0,2,1:T(8,128)(2,1)}, bf16[2,2,2,64,256]{4,3,0,2,1:T(8,128)(2,1)}, u32[]{:S(2)}, u32[]{:S(2)}) collective-permute-start(bf16[2,2,2,64,256]{4,3,0,2,1:T(8,128)(2,1)} %fusion.89), channel_id=1, source_target_pairs={{0,2},{2,4},{4,6},{6,8},{8,10},{10,12},{12,14},{14,16},{16,18},{18... | collective-permute-start | bytes 786440 | tf_op jit(solution)/shard_map/ppermute | solution.py:22
  816.0 14.6 %collective-permute-start.14 = (bf16[2,2,2,64,256]{4,3,0,2,1:T(8,128)(2,1)}, bf16[2,2,2,64,256]{4,3,0,2,1:T(8,128)(2,1)S(1)}, u32[]{:S(2)}, u32[]{:S(2)}) collective-permute-start(bf16[2,2,2,64,256]{4,3,0,2,1:T(8,128)(2,1)} %fusion.89), channel_id=1, source_target_pairs={{0,254},{2,0},{4,2},{6,4},{8,6},{10,8},{12,10},{14,12},{16,14},{18... | collective-permute-start | bytes 786440 | tf_op jit(solution)/shard_map/ppermute | solution.py:22
  830.6 20.3 %collective-permute-start.11 = (bf16[2,2,2,64,256]{4,3,0,2,1:T(8,128)(2,1)}, bf16[2,2,2,64,256]{4,3,0,2,1:T(8,128)(2,1)S(1)}, u32[]{:S(2)}, u32[]{:S(2)}) collective-permute-start(bf16[2,2,2,64,256]{4,3,0,2,1:T(8,128)(2,1)} %collective-permute-done.8), channel_id=1, source_target_pairs={{0,2},{2,4},{4,6},{6,8},{8,10},{10,12},{12,14},{14,16},{16,18},{18... | collective-permute-start | bytes 786440 | tf_op jit(solution)/shard_map/ppermute | solution.py:22
  845.6 17.6 %collective-permute-start.17 = (bf16[2,2,2,64,256]{4,3,0,2,1:T(8,128)(2,1)S(1)}, bf16[2,2,2,64,256]{4,3,0,2,1:T(8,128)(2,1)S(1)}, u32[]{:S(2)}, u32[]{:S(2)}) collective-permute-start(bf16[2,2,2,64,256]{4,3,0,2,1:T(8,128)(2,1)S(1)} %collective-permute-done.14), channel_id=1, source_target_pairs={{0,254},{2,0},{4,2},{6,4},{8,6},{10,8},{12,10},{14,12},{16,14},{18... | collective-permute-start | bytes 786440 | tf_op jit(solution)/shard_map/ppermute | solution.py:22
  1014.4 10.3 collective-permute-start.23
  1024.7 17.5 %collective-permute-start.24 = (bf16[2,2,2,64,128]{4,3,0,2,1:T(8,128)(2,1)S(1)}, bf16[2,2,2,64,128]{4,3,0,2,1:T(8,128)(2,1)S(1)}, u32[]{:S(2)}, u32[]{:S(2)}) collective-permute-start(bf16[2,2,2,64,128]{4,3,0,2,1:T(8,128)(2,1)S(1)} %collective-permute-done.23), channel_id=1, source_target_pairs={{0,16},{16,0},{2,18},{18,2},{4,20},{20,4},{6,22},{22,6},{8,24},{24... | collective-permute-start | bytes 393224 | tf_op jit(solution)/shard_map/ppermute | solution.py:17
  1042.2 24.1 %collective-permute-start.25 = (bf16[2,2,2,64,128]{4,3,0,2,1:T(8,128)(2,1)S(1)}, bf16[2,2,2,64,128]{4,3,0,2,1:T(8,128)(2,1)S(1)}, u32[]{:S(2)}, u32[]{:S(2)}) collective-permute-start(bf16[2,2,2,64,128]{4,3,0,2,1:T(8,128)(2,1)S(1)} %collective-permute-done.24), channel_id=1, source_target_pairs={{0,32},{32,0},{2,34},{34,2},{4,36},{36,4},{6,38},{38,6},{8,40},{40... | collective-permute-start | bytes 393224 | tf_op jit(solution)/shard_map/ppermute | solution.py:17
  1073.2 8.4 collective-permute-start.27
  (65 other events, 1564.9 us)
Sparse Core Ops, SparseCore 0:
  901.9 92.3 reduce-scatter.3
where the time goes:
time: 1100 us; the launch traced here: 1090 us
  blocking collectives  583 us (53%)
  waiting for transfers between devices  201 us (18%)
  starting transfers between devices  120 us (11%)
  matrix products  76.2 us (7%)
  other arithmetic  56.5 us (5%)
  local copies, waits for them, and re-layouts  38.9 us (4%)
  between operations  15.1 us (1%)
    psum x1, blocking collectives, per_device(): spread = lax.psum(spread, ('ka', 'isdf'))  583 us
    ppermute x16, waiting for transfers between devices, swapped(): return lax.ppermute(block, axis, route)  108 us
    unnamed x2, waiting for transfers between devices  92.5 us
    ppermute x16, starting transfers between devices, swapped(): return lax.ppermute(block, axis, route)  71.8 us
    dot_general x48, matrix products, single(): jnp.einsum(pattern, first, second, preferred_element_type=jnp.float32)  53.3 us
    ppermute x12, starting transfers between devices, shifted(): lax.ppermute(value, axis, [(i, (i + by) % size) for i in range(size)])  47.7 us
    dot_general x10, matrix products, accumulate(): jnp.einsum('kw,wrmn->rkmn', selector[:, visitor], screened, preferred_ele...  22.4 us
  transfers between devices with their start and end apart: 29, of which 14 were waited for; matrix products, arithmetic and copies ran while one was open for 12% of the time, Pallas kernels for 0%

commit v1 on v0

--- a/solution.py
+++ b/solution.py
@@ -96,7 +96,7 @@
     )
     density = jnp.stack([rho_real, rho_imag], axis=1)
     spread = jnp.einsum("nm,brm->brn", coulomb, density, precision=HIGHEST)
-    spread = lax.psum(spread, ("ka", "isdf"))
+    spread = jnp.sum(lax.all_gather(spread, ("ka", "isdf")), axis=0)
     potential = lax.dynamic_slice_in_dim(spread, isdf_index * mu_count, mu_count, 2)
     class_ids = jnp.arange(screened.shape[0], dtype=jnp.int32)
 

time: 1100 us -> 553 us (0.50)
  blocking collectives: 583 us -> 0 us
  waiting for transfers between devices: 201 us -> 227 us
    psum x1 -> x0, blocking collectives: 583 us -> none  [per_device(): spread = lax.psum(spread, ('ka', 'isdf'))]
    all_gather x0 -> x1, waiting for transfers between devices: none -> 99.4 us  [per_device(): spread = jnp.sum(lax.all_gather(spread, ('ka', 'isdf')), axis=0)]
    unnamed x2 -> x3, waiting for transfers between devices: 92.5 us -> 18.7 us
  transfers between devices with their start and end apart: 29 -> 30, of which waited for: 14 -> 15; matrix products, arithmetic and copies ran while one was open for 12% -> 31% of each run, Pallas kernels for 0% -> 0%
where the time goes in v1:
time: 553 us; the launch traced here: 542 us
  waiting for transfers between devices  227 us (41%)
  starting transfers between devices  123 us (22%)
  matrix products  78.7 us (14%)
  other arithmetic  58.7 us (11%)
  local copies, waits for them, and re-layouts  39.5 us (7%)
  between operations  15.1 us (3%)
    ppermute x16, waiting for transfers between devices, swapped(): return lax.ppermute(block, axis, route)  108 us
    all_gather x1, waiting for transfers between devices, per_device(): spread = jnp.sum(lax.all_gather(spread, ('ka', 'isdf')), axis=0)  99.4 us
    ppermute x16, starting transfers between devices, swapped(): return lax.ppermute(block, axis, route)  71.7 us
    dot_general x48, matrix products, single(): jnp.einsum(pattern, first, second, preferred_element_type=jnp.float32)  54.8 us
    ppermute x12, starting transfers between devices, shifted(): lax.ppermute(value, axis, [(i, (i + by) % size) for i in range(size)])  51.5 us
    dot_general x10, matrix products, accumulate(): jnp.einsum('kw,wrmn->rkmn', selector[:, visitor], screened, preferred_ele...  22.8 us
    mul x10, other arithmetic, accumulate(): screen_real * visit_real - screen_imag * visit_imag  21.5 us
    unnamed x3, waiting for transfers between devices  18.7 us
  transfers between devices with their start and end apart: 30, of which 15 were waited for; matrix products, arithmetic and copies ran while one was open for 31% of the time, Pallas kernels for 0%

profile of v1, /device:TPU:2, one launch (start us, length us, event | category | flops | bytes accessed | tf_op | source)
XLA Modules:
  0.0 541.9 jit_solution(15929999312341073955)
XLA Ops:
  8.6 10.8 %collective-permute-start.15 = (bf16[2,2,256,256]{3,2,1,0:T(8,128)(2,1)}, bf16[2,2,256,256]{3,2,1,0:T(8,128)(2,1)}, u32[]{:S(2)}, u32[]{:S(2)}) collective-permute-start(bf16[2,2,256,256]{3,2,1,0:T(8,128)(2,1)} %param.9), channel_id=1, source_target_pairs={{0,254},{2,0},{4,2},{6,4},{8,6},{10,8},{12,10},{14,12},{16,14},{18... | collective-permute-start | bytes 1572872 | tf_op jit(solution)/shard_map/ppermute | solution.py:22
  21.3 5.8 %collective-permute-start.16 = (bf16[2,2,64,512]{3,2,1,0:T(8,128)(2,1)}, bf16[2,2,64,512]{3,2,1,0:T(8,128)(2,1)}, u32[]{:S(2)}, u32[]{:S(2)}) collective-permute-start(bf16[2,2,64,512]{3,2,1,0:T(8,128)(2,1)} %param.10), channel_id=1, source_target_pairs={{0,254},{2,0},{4,2},{6,4},{8,6},{10,8},{12,10},{14,12},{16,14},{18... | collective-permute-start | bytes 786440 | tf_op jit(solution)/shard_map/ppermute | solution.py:22
  77.7 6.6 %collective-permute-done.2 = bf16[2,2,2,64,256]{4,3,0,2,1:T(8,128)(2,1)S(1)} collective-permute-done((bf16[2,2,2,64,256]{4,3,0,2,1:T(8,128)(2,1)S(1)}, bf16[2,2,2,64,256]{4,3,0,2,1:T(8,128)(2,1)S(1)}, u32[]{:S(2)}, u32[]{:S(2)}) %collective-permute-start.2) | collective-permute-done | bytes 262176 | tf_op jit(solution)/shard_map/ppermute | solution.py:17
  88.3 12.3 %collective-permute-done.3 = bf16[2,2,2,64,256]{4,3,0,2,1:T(8,128)(2,1)S(1)} collective-permute-done((bf16[2,2,2,64,256]{4,3,0,2,1:T(8,128)(2,1)S(1)}, bf16[2,2,2,64,256]{4,3,0,2,1:T(8,128)(2,1)S(1)}, u32[]{:S(2)}, u32[]{:S(2)}) %collective-permute-start.3) | collective-permute-done | bytes 262176 | tf_op jit(solution)/shard_map/ppermute | solution.py:17
  105.1 22.7 %collective-permute-done.4 = bf16[2,2,2,64,256]{4,3,0,2,1:T(8,128)(2,1)S(1)} collective-permute-done((bf16[2,2,2,64,256]{4,3,0,2,1:T(8,128)(2,1)S(1)}, bf16[2,2,2,64,256]{4,3,0,2,1:T(8,128)(2,1)S(1)}, u32[]{:S(2)}, u32[]{:S(2)}) %collective-permute-start.4) | collective-permute-done | bytes 262176 | tf_op jit(solution)/shard_map/ppermute | solution.py:17
  127.7 14.7 %collective-permute-start.5 = (bf16[2,2,2,64,256]{4,3,0,2,1:T(8,128)(2,1)S(1)}, bf16[2,2,2,64,256]{4,3,0,2,1:T(8,128)(2,1)S(1)}, u32[]{:S(2)}, u32[]{:S(2)}) collective-permute-start(bf16[2,2,2,64,256]{4,3,0,2,1:T(8,128)(2,1)S(1)} %collective-permute-done.4), channel_id=1, source_target_pairs={{0,32},{32,0},{2,34},{34,2},{4,36},{36,4},{6,38},{38,6},{8,40},{40... | collective-permute-start | bytes 786440 | tf_op jit(solution)/shard_map/ppermute | solution.py:17
  144.4 14.9 %collective-permute-done.5 = bf16[2,2,2,64,256]{4,3,0,2,1:T(8,128)(2,1)S(1)} collective-permute-done((bf16[2,2,2,64,256]{4,3,0,2,1:T(8,128)(2,1)S(1)}, bf16[2,2,2,64,256]{4,3,0,2,1:T(8,128)(2,1)S(1)}, u32[]{:S(2)}, u32[]{:S(2)}) %collective-permute-start.5) | collective-permute-done | bytes 262176 | tf_op jit(solution)/shard_map/ppermute | solution.py:17
  164.1 5.4 collective-permute-done.6
  199.7 5.8 %collective-permute-start.19 = (bf16[2,2,64,512]{3,2,1,0:T(8,128)(2,1)}, bf16[2,2,64,512]{3,2,1,0:T(8,128)(2,1)}, u32[]{:S(2)}, u32[]{:S(2)}) collective-permute-start(bf16[2,2,64,512]{3,2,1,0:T(8,128)(2,1)} %collective-permute-done.16), channel_id=1, source_target_pairs={{0,254},{2,0},{4,2},{6,4},{8,6},{10,8},{12,10},{14,12},{16,14},{18... | collective-permute-start | bytes 786440 | tf_op jit(solution)/shard_map/ppermute | solution.py:22
  207.5 5.8 %collective-permute-start.18 = (bf16[2,2,256,256]{3,2,1,0:T(8,128)(2,1)}, bf16[2,2,256,256]{3,2,1,0:T(8,128)(2,1)}, u32[]{:S(2)}, u32[]{:S(2)}) collective-permute-start(bf16[2,2,256,256]{3,2,1,0:T(8,128)(2,1)} %collective-permute-done.15), channel_id=1, source_target_pairs={{0,254},{2,0},{4,2},{6,4},{8,6},{10,8},{12,10},{14,12},{16,14},{18... | collective-permute-start | bytes 1572872 | tf_op jit(solution)/shard_map/ppermute | solution.py:22
  234.6 5.8 %collective-permute-start.14 = (bf16[2,2,2,64,256]{4,3,0,2,1:T(8,128)(2,1)}, bf16[2,2,2,64,256]{4,3,0,2,1:T(8,128)(2,1)S(1)}, u32[]{:S(2)}, u32[]{:S(2)}) collective-permute-start(bf16[2,2,2,64,256]{4,3,0,2,1:T(8,128)(2,1)} %fusion.89), channel_id=1, source_target_pairs={{0,254},{2,0},{4,2},{6,4},{8,6},{10,8},{12,10},{14,12},{16,14},{18... | collective-permute-start | bytes 786440 | tf_op jit(solution)/shard_map/ppermute | solution.py:22
  267.5 6.0 %collective-permute-start.17 = (bf16[2,2,2,64,256]{4,3,0,2,1:T(8,128)(2,1)S(1)}, bf16[2,2,2,64,256]{4,3,0,2,1:T(8,128)(2,1)S(1)}, u32[]{:S(2)}, u32[]{:S(2)}) collective-permute-start(bf16[2,2,2,64,256]{4,3,0,2,1:T(8,128)(2,1)S(1)} %collective-permute-done.14), channel_id=1, source_target_pairs={{0,254},{2,0},{4,2},{6,4},{8,6},{10,8},{12,10},{14,12},{16,14},{18... | collective-permute-start | bytes 786440 | tf_op jit(solution)/shard_map/ppermute | solution.py:22
  301.2 9.3 %add_convert_fusion.1 = bf16[2,2,256,512]{3,2,0,1:T(8,128)(2,1)S(1)} fusion(f32[2,256,512]{2,1,0:T(8,128)} %get-tuple-element.48, f32[2,256,512]{2,1,0:T(8,128)S(1)} %copy-done.14, f32[2,256,512]{2,1,0:T(8,128)} %get-tuple-element.69, f32[2,256,512]{2,1,0:T(8,128)S(1)} %copy-done.13, f32[2,256,512]{2,1,0:T(8,128)} %get-tuple-element.47, ...), kind=kLoop, calls=%fused_computation.3 | loop fusion | flops 20971520 | bytes 42991616 | tf_op jit(solution)/shard_map/convert_element_type | solution.py:150
  312.7 9.5 %add_convert_fusion = bf16[2,2,256,512]{3,2,0,1:T(8,128)(2,1)S(1)} fusion(f32[2,256,512]{2,1,0:T(8,128)} %get-tuple-element.48, f32[2,256,512]{2,1,0:T(8,128)S(1)} %copy-done.14, f32[2,256,512]{2,1,0:T(8,128)} %get-tuple-element.69, f32[2,256,512]{2,1,0:T(8,128)S(1)} %copy-done.13, f32[2,256,512]{2,1,0:T(8,128)} %get-tuple-element.47, ...), kind=kLoop, calls=%fused_computation.2 | loop fusion | flops 20971520 | bytes 42991616 | tf_op jit(solution)/shard_map/convert_element_type | solution.py:151
  322.2 99.4 %all-gather.3.cloned.1.call-done = f32[512,2,512]{2,1,0:T(2,128)} async-done(((f32[2,2,512]{2,1,0:T(2,128)}), f32[512,2,512]{2,1,0:T(2,128)}) %all-gather.3.cloned.1.call-update) | async-done | bytes 2097168 | tf_op jit(solution)/shard_map/all_gather | solution.py:99
  427.3 18.7 %reduce-scatter.4.cloned.1.call-done = bf16[128,512]{1,0:T(8,128)(2,1)} async-done(((bf16[256,512]{1,0:T(8,128)(2,1)}), bf16[128,512]{1,0:T(8,128)(2,1)}) %reduce-scatter.4.cloned.1.call-update) | async-done | bytes 131088
  450.8 4.6 collective-permute-done.20
  466.2 4.4 collective-permute-start.23
  470.6 5.9 %collective-permute-done.23 = bf16[2,2,2,64,128]{4,3,0,2,1:T(8,128)(2,1)S(1)} collective-permute-done((bf16[2,2,2,64,128]{4,3,0,2,1:T(8,128)(2,1)S(1)}, bf16[2,2,2,64,128]{4,3,0,2,1:T(8,128)(2,1)S(1)}, u32[]{:S(2)}, u32[]{:S(2)}) %collective-permute-start.23) | collective-permute-done | bytes 131104 | tf_op jit(solution)/shard_map/ppermute | solution.py:17
  476.5 7.6 %collective-permute-start.24 = (bf16[2,2,2,64,128]{4,3,0,2,1:T(8,128)(2,1)S(1)}, bf16[2,2,2,64,128]{4,3,0,2,1:T(8,128)(2,1)S(1)}, u32[]{:S(2)}, u32[]{:S(2)}) collective-permute-start(bf16[2,2,2,64,128]{4,3,0,2,1:T(8,128)(2,1)S(1)} %collective-permute-done.23), channel_id=1, source_target_pairs={{0,16},{16,0},{2,18},{18,2},{4,20},{20,4},{6,22},{22,6},{8,24},{24... | collective-permute-start | bytes 393224 | tf_op jit(solution)/shard_map/ppermute | solution.py:17
  484.1 9.9 %collective-permute-done.24 = bf16[2,2,2,64,128]{4,3,0,2,1:T(8,128)(2,1)S(1)} collective-permute-done((bf16[2,2,2,64,128]{4,3,0,2,1:T(8,128)(2,1)S(1)}, bf16[2,2,2,64,128]{4,3,0,2,1:T(8,128)(2,1)S(1)}, u32[]{:S(2)}, u32[]{:S(2)}) %collective-permute-start.24) | collective-permute-done | bytes 131104 | tf_op jit(solution)/shard_map/ppermute | solution.py:17
  494.0 12.0 %collective-permute-start.25 = (bf16[2,2,2,64,128]{4,3,0,2,1:T(8,128)(2,1)S(1)}, bf16[2,2,2,64,128]{4,3,0,2,1:T(8,128)(2,1)S(1)}, u32[]{:S(2)}, u32[]{:S(2)}) collective-permute-start(bf16[2,2,2,64,128]{4,3,0,2,1:T(8,128)(2,1)S(1)} %collective-permute-done.24), channel_id=1, source_target_pairs={{0,32},{32,0},{2,34},{34,2},{4,36},{36,4},{6,38},{38,6},{8,40},{40... | collective-permute-start | bytes 393224 | tf_op jit(solution)/shard_map/ppermute | solution.py:17
  506.0 12.1 %collective-permute-done.25 = bf16[2,2,2,64,128]{4,3,0,2,1:T(8,128)(2,1)S(1)} collective-permute-done((bf16[2,2,2,64,128]{4,3,0,2,1:T(8,128)(2,1)S(1)}, bf16[2,2,2,64,128]{4,3,0,2,1:T(8,128)(2,1)S(1)}, u32[]{:S(2)}, u32[]{:S(2)}) %collective-permute-start.25) | collective-permute-done | bytes 131104 | tf_op jit(solution)/shard_map/ppermute | solution.py:17
  520.4 4.5 collective-permute-done.26
  (302 shorter events, 212.7 us)
Async XLA Ops:
  6.5 415.1 %all-gather.3.cloned.1.call-start = ((), (), s32[]{:S(2)}) async-start(), calls=%async_computation.1 | async-start | bytes 2105344 | tf_op jit(solution)/shard_map/all_gather | solution.py:99
  6.5 199.0 %collective-permute-start.9 = (bf16[2,2,256,256]{3,2,1,0:T(8,128)(2,1)}, bf16[2,2,256,256]{3,2,1,0:T(8,128)(2,1)}, u32[]{:S(2)}, u32[]{:S(2)}) collective-permute-start(bf16[2,2,256,256]{3,2,1,0:T(8,128)(2,1)} %param.9), channel_id=1, source_target_pairs={{0,2},{2,4},{4,6},{6,8},{8,10},{10,12},{12,14},{14,16},{16,18},{18... | collective-permute-start | bytes 1572872 | tf_op jit(solution)/shard_map/ppermute | solution.py:22
  8.6 198.9 %collective-permute-start.15 = (bf16[2,2,256,256]{3,2,1,0:T(8,128)(2,1)}, bf16[2,2,256,256]{3,2,1,0:T(8,128)(2,1)}, u32[]{:S(2)}, u32[]{:S(2)}) collective-permute-start(bf16[2,2,256,256]{3,2,1,0:T(8,128)(2,1)} %param.9), channel_id=1, source_target_pairs={{0,254},{2,0},{4,2},{6,4},{8,6},{10,8},{12,10},{14,12},{16,14},{18... | collective-permute-start | bytes 1572872 | tf_op jit(solution)/shard_map/ppermute | solution.py:22
  19.4 178.3 %collective-permute-start.10 = (bf16[2,2,64,512]{3,2,1,0:T(8,128)(2,1)}, bf16[2,2,64,512]{3,2,1,0:T(8,128)(2,1)}, u32[]{:S(2)}, u32[]{:S(2)}) collective-permute-start(bf16[2,2,64,512]{3,2,1,0:T(8,128)(2,1)} %param.10), channel_id=1, source_target_pairs={{0,2},{2,4},{4,6},{6,8},{8,10},{10,12},{12,14},{14,16},{16,18},{18... | collective-permute-start | bytes 786440 | tf_op jit(solution)/shard_map/ppermute | solution.py:22
  21.3 178.4 %collective-permute-start.16 = (bf16[2,2,64,512]{3,2,1,0:T(8,128)(2,1)}, bf16[2,2,64,512]{3,2,1,0:T(8,128)(2,1)}, u32[]{:S(2)}, u32[]{:S(2)}) collective-permute-start(bf16[2,2,64,512]{3,2,1,0:T(8,128)(2,1)} %param.10), channel_id=1, source_target_pairs={{0,254},{2,0},{4,2},{6,4},{8,6},{10,8},{12,10},{14,12},{16,14},{18... | collective-permute-start | bytes 786440 | tf_op jit(solution)/shard_map/ppermute | solution.py:22
  28.8 40.6 %collective-permute-start = (bf16[2,2,2,64,256]{4,3,0,2,1:T(8,128)(2,1)}, bf16[2,2,2,64,256]{4,3,0,2,1:T(8,128)(2,1)S(1)}, u32[]{:S(2)}, u32[]{:S(2)}) collective-permute-start(bf16[2,2,2,64,256]{4,3,0,2,1:T(8,128)(2,1)} %bitcast.647), channel_id=1, source_target_pairs={{0,256},{256,0},{1,257},{257,1},{2,258},{258,2},{3,259},{259,3},{4... | collective-permute-start | bytes 786440 | tf_op jit(solution)/shard_map/ppermute | solution.py:17
  73.6 10.7 %collective-permute-start.2 = (bf16[2,2,2,64,256]{4,3,0,2,1:T(8,128)(2,1)S(1)}, bf16[2,2,2,64,256]{4,3,0,2,1:T(8,128)(2,1)S(1)}, u32[]{:S(2)}, u32[]{:S(2)}) collective-permute-start(bf16[2,2,2,64,256]{4,3,0,2,1:T(8,128)(2,1)S(1)} %collective-permute-done.1), channel_id=1, source_target_pairs={{0,4},{4,0},{2,6},{6,2},{8,12},{12,8},{10,14},{14,10},{16,20},{20,... | collective-permute-start | bytes 786440 | tf_op jit(solution)/shard_map/ppermute | solution.py:17
  84.3 16.3 %collective-permute-start.3 = (bf16[2,2,2,64,256]{4,3,0,2,1:T(8,128)(2,1)S(1)}, bf16[2,2,2,64,256]{4,3,0,2,1:T(8,128)(2,1)S(1)}, u32[]{:S(2)}, u32[]{:S(2)}) collective-permute-start(bf16[2,2,2,64,256]{4,3,0,2,1:T(8,128)(2,1)S(1)} %collective-permute-done.2), channel_id=1, source_target_pairs={{0,8},{8,0},{2,10},{10,2},{4,12},{12,4},{6,14},{14,6},{16,24},{24,... | collective-permute-start | bytes 786440 | tf_op jit(solution)/shard_map/ppermute | solution.py:17
  100.6 27.1 %collective-permute-start.4 = (bf16[2,2,2,64,256]{4,3,0,2,1:T(8,128)(2,1)S(1)}, bf16[2,2,2,64,256]{4,3,0,2,1:T(8,128)(2,1)S(1)}, u32[]{:S(2)}, u32[]{:S(2)}) collective-permute-start(bf16[2,2,2,64,256]{4,3,0,2,1:T(8,128)(2,1)S(1)} %collective-permute-done.3), channel_id=1, source_target_pairs={{0,16},{16,0},{2,18},{18,2},{4,20},{20,4},{6,22},{22,6},{8,24},{24... | collective-permute-start | bytes 786440 | tf_op jit(solution)/shard_map/ppermute | solution.py:17
  127.7 31.6 %collective-permute-start.5 = (bf16[2,2,2,64,256]{4,3,0,2,1:T(8,128)(2,1)S(1)}, bf16[2,2,2,64,256]{4,3,0,2,1:T(8,128)(2,1)S(1)}, u32[]{:S(2)}, u32[]{:S(2)}) collective-permute-start(bf16[2,2,2,64,256]{4,3,0,2,1:T(8,128)(2,1)S(1)} %collective-permute-done.4), channel_id=1, source_target_pairs={{0,32},{32,0},{2,34},{34,2},{4,36},{36,4},{6,38},{38,6},{8,40},{40... | collective-permute-start | bytes 786440 | tf_op jit(solution)/shard_map/ppermute | solution.py:17
  159.3 10.2 %collective-permute-start.6 = (bf16[2,2,2,64,256]{4,3,0,2,1:T(8,128)(2,1)S(1)}, bf16[2,2,2,64,256]{4,3,0,2,1:T(8,128)(2,1)}, u32[]{:S(2)}, u32[]{:S(2)}) collective-permute-start(bf16[2,2,2,64,256]{4,3,0,2,1:T(8,128)(2,1)S(1)} %collective-permute-done.5), channel_id=1, source_target_pairs={{0,64},{64,0},{2,66},{66,2},{4,68},{68,4},{6,70},{70,6},{8,72},{72... | collective-permute-start | bytes 786440 | tf_op jit(solution)/shard_map/ppermute | solution.py:17
  169.5 43.7 %collective-permute-start.7 = (bf16[2,2,2,64,256]{4,3,0,2,1:T(8,128)(2,1)}, bf16[2,2,2,64,256]{4,3,0,2,1:T(8,128)(2,1)}, u32[]{:S(2)}, u32[]{:S(2)}) collective-permute-start(bf16[2,2,2,64,256]{4,3,0,2,1:T(8,128)(2,1)} %collective-permute-done.6), channel_id=1, source_target_pairs={{0,128},{128,0},{2,130},{130,2},{4,132},{132,4},{6,134},{134,6},{8... | collective-permute-start | bytes 786440 | tf_op jit(solution)/shard_map/ppermute | solution.py:17
  197.7 80.4 %collective-permute-start.13 = (bf16[2,2,64,512]{3,2,1,0:T(8,128)(2,1)}, bf16[2,2,64,512]{3,2,1,0:T(8,128)(2,1)}, u32[]{:S(2)}, u32[]{:S(2)}) collective-permute-start(bf16[2,2,64,512]{3,2,1,0:T(8,128)(2,1)} %collective-permute-done.10), channel_id=1, source_target_pairs={{0,2},{2,4},{4,6},{6,8},{8,10},{10,12},{12,14},{14,16},{16,18},{18... | collective-permute-start | bytes 786440 | tf_op jit(solution)/shard_map/ppermute | solution.py:22
  199.7 90.8 %collective-permute-start.19 = (bf16[2,2,64,512]{3,2,1,0:T(8,128)(2,1)}, bf16[2,2,64,512]{3,2,1,0:T(8,128)(2,1)}, u32[]{:S(2)}, u32[]{:S(2)}) collective-permute-start(bf16[2,2,64,512]{3,2,1,0:T(8,128)(2,1)} %collective-permute-done.16), channel_id=1, source_target_pairs={{0,254},{2,0},{4,2},{6,4},{8,6},{10,8},{12,10},{14,12},{16,14},{18... | collective-permute-start | bytes 786440 | tf_op jit(solution)/shard_map/ppermute | solution.py:22
  205.5 62.0 %collective-permute-start.12 = (bf16[2,2,256,256]{3,2,1,0:T(8,128)(2,1)}, bf16[2,2,256,256]{3,2,1,0:T(8,128)(2,1)}, u32[]{:S(2)}, u32[]{:S(2)}) collective-permute-start(bf16[2,2,256,256]{3,2,1,0:T(8,128)(2,1)} %collective-permute-done.9), channel_id=1, source_target_pairs={{0,2},{2,4},{4,6},{6,8},{8,10},{10,12},{12,14},{14,16},{16,18},{18... | collective-permute-start | bytes 1572872 | tf_op jit(solution)/shard_map/ppermute | solution.py:22
  207.5 78.4 %collective-permute-start.18 = (bf16[2,2,256,256]{3,2,1,0:T(8,128)(2,1)}, bf16[2,2,256,256]{3,2,1,0:T(8,128)(2,1)}, u32[]{:S(2)}, u32[]{:S(2)}) collective-permute-start(bf16[2,2,256,256]{3,2,1,0:T(8,128)(2,1)} %collective-permute-done.15), channel_id=1, source_target_pairs={{0,254},{2,0},{4,2},{6,4},{8,6},{10,8},{12,10},{14,12},{16,14},{18... | collective-permute-start | bytes 1572872 | tf_op jit(solution)/shard_map/ppermute | solution.py:22
  222.2 12.4 %collective-permute-start.8 = (bf16[2,2,2,64,256]{4,3,0,2,1:T(8,128)(2,1)}, bf16[2,2,2,64,256]{4,3,0,2,1:T(8,128)(2,1)}, u32[]{:S(2)}, u32[]{:S(2)}) collective-permute-start(bf16[2,2,2,64,256]{4,3,0,2,1:T(8,128)(2,1)} %fusion.89), channel_id=1, source_target_pairs={{0,2},{2,4},{4,6},{6,8},{8,10},{10,12},{12,14},{14,16},{16,18},{18... | collective-permute-start | bytes 786440 | tf_op jit(solution)/shard_map/ppermute | solution.py:22
  230.1 216.0 %reduce-scatter.4.cloned.1.call-start = ((), (), s32[]{:S(2)}) async-start(), calls=%async_computation.2 | async-start | bytes 393216
  234.6 18.5 %collective-permute-start.14 = (bf16[2,2,2,64,256]{4,3,0,2,1:T(8,128)(2,1)}, bf16[2,2,2,64,256]{4,3,0,2,1:T(8,128)(2,1)S(1)}, u32[]{:S(2)}, u32[]{:S(2)}) collective-permute-start(bf16[2,2,2,64,256]{4,3,0,2,1:T(8,128)(2,1)} %fusion.89), channel_id=1, source_target_pairs={{0,254},{2,0},{4,2},{6,4},{8,6},{10,8},{12,10},{14,12},{16,14},{18... | collective-permute-start | bytes 786440 | tf_op jit(solution)/shard_map/ppermute | solution.py:22
  253.1 20.4 %collective-permute-start.11 = (bf16[2,2,2,64,256]{4,3,0,2,1:T(8,128)(2,1)}, bf16[2,2,2,64,256]{4,3,0,2,1:T(8,128)(2,1)S(1)}, u32[]{:S(2)}, u32[]{:S(2)}) collective-permute-start(bf16[2,2,2,64,256]{4,3,0,2,1:T(8,128)(2,1)} %collective-permute-done.8), channel_id=1, source_target_pairs={{0,2},{2,4},{4,6},{6,8},{8,10},{10,12},{12,14},{14,16},{16,18},{18... | collective-permute-start | bytes 786440 | tf_op jit(solution)/shard_map/ppermute | solution.py:22
  267.5 18.3 %collective-permute-start.17 = (bf16[2,2,2,64,256]{4,3,0,2,1:T(8,128)(2,1)S(1)}, bf16[2,2,2,64,256]{4,3,0,2,1:T(8,128)(2,1)S(1)}, u32[]{:S(2)}, u32[]{:S(2)}) collective-permute-start(bf16[2,2,2,64,256]{4,3,0,2,1:T(8,128)(2,1)S(1)} %collective-permute-done.14), channel_id=1, source_target_pairs={{0,254},{2,0},{4,2},{6,4},{8,6},{10,8},{12,10},{14,12},{16,14},{18... | collective-permute-start | bytes 786440 | tf_op jit(solution)/shard_map/ppermute | solution.py:22
  466.2 10.3 %collective-permute-start.23 = (bf16[2,2,2,64,128]{4,3,0,2,1:T(8,128)(2,1)S(1)}, bf16[2,2,2,64,128]{4,3,0,2,1:T(8,128)(2,1)S(1)}, u32[]{:S(2)}, u32[]{:S(2)}) collective-permute-start(bf16[2,2,2,64,128]{4,3,0,2,1:T(8,128)(2,1)S(1)} %collective-permute-done.22), channel_id=1, source_target_pairs={{0,8},{8,0},{2,10},{10,2},{4,12},{12,4},{6,14},{14,6},{16,24},{24,... | collective-permute-start | bytes 393224 | tf_op jit(solution)/shard_map/ppermute | solution.py:17
  476.5 17.5 %collective-permute-start.24 = (bf16[2,2,2,64,128]{4,3,0,2,1:T(8,128)(2,1)S(1)}, bf16[2,2,2,64,128]{4,3,0,2,1:T(8,128)(2,1)S(1)}, u32[]{:S(2)}, u32[]{:S(2)}) collective-permute-start(bf16[2,2,2,64,128]{4,3,0,2,1:T(8,128)(2,1)S(1)} %collective-permute-done.23), channel_id=1, source_target_pairs={{0,16},{16,0},{2,18},{18,2},{4,20},{20,4},{6,22},{22,6},{8,24},{24... | collective-permute-start | bytes 393224 | tf_op jit(solution)/shard_map/ppermute | solution.py:17
  494.0 24.1 %collective-permute-start.25 = (bf16[2,2,2,64,128]{4,3,0,2,1:T(8,128)(2,1)S(1)}, bf16[2,2,2,64,128]{4,3,0,2,1:T(8,128)(2,1)S(1)}, u32[]{:S(2)}, u32[]{:S(2)}) collective-permute-start(bf16[2,2,2,64,128]{4,3,0,2,1:T(8,128)(2,1)S(1)} %collective-permute-done.24), channel_id=1, source_target_pairs={{0,32},{32,0},{2,34},{34,2},{4,36},{36,4},{6,38},{38,6},{8,40},{40... | collective-permute-start | bytes 393224 | tf_op jit(solution)/shard_map/ppermute | solution.py:17
  (69 other events, 1257.1 us)
Sparse Core Ops, SparseCore 0:
  230.2 191.3 all-gather.2
  427.5 18.5 reduce-scatter.3
